TPU v7x, 256 devices: a whole 4x4x8 slice. The times are simulated.
256 devices in a mesh: dp: 32 (over y, z_lo, core), layer: 8 (over z_hi, x).
Axes of the slice: x: 4, y: 4, z: 8 (z_hi: 2, z_lo: 4; z = z_hi * 4 + z_lo), core: 2. Of those that a mesh axis runs over, the one named last changes fastest.
Arguments:
- hidden: bfloat16 [4096, 8192], P('dp'), may hold values from -0.29882812 to 0.29882812
- w_kv: bfloat16 [8, 8192, 1024], P('layer', 'dp'), may hold values from -0.0625 to 0.0625
- queries: bfloat16 [8, 4096, 4096], P('layer', 'dp'), may hold values from -128 to 128
- keys: bfloat16 [8, 4096, 512], P('layer', 'dp'), may hold values from -6 to 6
- values: bfloat16 [8, 4096, 512], P('layer', 'dp'), may hold values from -6 to 6
- out_grad: bfloat16 [8, 4096, 4096], P('layer', 'dp'), may hold values from -6 to 6
- doc_lengths: int32 [32, 8], P('dp'), may hold values from 1 to 64, 128 in all within a row
Outputs:
- grad_hidden: bfloat16 [4096, 8192], P('dp', 'layer')
- grad_w: bfloat16 [8, 8192, 1024], P('layer', 'dp')
Inputs may be any that keep to these rules, and one draw needn't show every extreme that they name: `doc_lengths`: each row sums to 128 and its largest entry is 64.
All inputs are finite; a program needn't handle non-finite values.
Results may differ from a plain program's by a relative error of at most 0.0076.
Values may be sent and summed in bfloat16 or wider, within the bound.
A program may use at most 128 MiB of HBM per device.

v0:
```python
import jax
import jax.numpy as jnp
from jax import lax
from jax.sharding import PartitionSpec as P

HEAD_SIZE = 128
KV_HEAD_COUNT = 4
QUERY_PER_KV = 8


def attend_back(query_block_tile, key_block_tile, value_block_tile, output_gradient_block, lengths):
    element_count = query_block_tile.shape[0]
    scale = HEAD_SIZE ** (-0.5)
    head_queries = query_block_tile.reshape(element_count, KV_HEAD_COUNT, QUERY_PER_KV, HEAD_SIZE)
    head_keys = key_block_tile.reshape(element_count, KV_HEAD_COUNT, HEAD_SIZE)
    head_values = value_block_tile.reshape(element_count, KV_HEAD_COUNT, HEAD_SIZE)
    output_gradient_head = output_gradient_block.reshape(
        element_count, KV_HEAD_COUNT, QUERY_PER_KV, HEAD_SIZE
    )
    position = jnp.arange(element_count, dtype=jnp.int32)
    ends = jnp.cumsum(lengths)
    doc_ids = jnp.sum((position[:, None] >= ends[None, :]).astype(jnp.int32), axis=1)
    allowed = (doc_ids[:, None] == doc_ids[None, :]) & (position[None, :] <= position[:, None])
    scores = (
        jnp.einsum("tkgd,skd->kgts", head_queries, head_keys, preferred_element_type=jnp.float32)
        * scale
    )
    scores = jnp.where(allowed[None, None], scores, jnp.float32(-1e30))
    top = jnp.max(scores, axis=-1, keepdims=True)
    expo = jnp.exp(scores - top)
    probs = expo / jnp.sum(expo, axis=-1, keepdims=True)
    probs_b = probs.astype(jnp.bfloat16)
    attn_out = jnp.einsum(
        "kgts,skd->tkgd", probs_b, head_values, preferred_element_type=jnp.float32
    )
    delta = jnp.transpose(
        jnp.sum(output_gradient_head.astype(jnp.float32) * attn_out, axis=-1), (1, 2, 0)
    )
    dprobs = jnp.einsum(
        "tkgd,skd->kgts", output_gradient_head, head_values, preferred_element_type=jnp.float32
    )
    dscores_b = (probs * (dprobs - delta[..., None])).astype(jnp.bfloat16)
    value_gradient = jnp.einsum(
        "kgts,tkgd->skd", probs_b, output_gradient_head, preferred_element_type=jnp.float32
    )
    key_gradient = (
        jnp.einsum("kgts,tkgd->skd", dscores_b, head_queries, preferred_element_type=jnp.float32)
        * scale
    )
    merged_gradient = jnp.concatenate(
        [
            key_gradient.reshape(element_count, KV_HEAD_COUNT * HEAD_SIZE),
            value_gradient.reshape(element_count, KV_HEAD_COUNT * HEAD_SIZE),
        ],
        axis=-1,
    )
    return merged_gradient.astype(jnp.bfloat16)


def local(hidden, w_kv, queries, keys, values, out_grad, doc_lengths):
    grads = [attend_back(queries[0], keys[0], values[0], out_grad[0], doc_lengths[0])]
    key_value_gradient = jnp.stack(grads, axis=0)
    columns = lax.all_to_all(hidden, "dp", split_axis=1, concat_axis=0, tiled=True)
    block = lax.all_gather(key_value_gradient, "dp", axis=1, tiled=True)
    row_terms = jnp.einsum("lnc,ldc->nd", block, w_kv, preferred_element_type=jnp.float32)
    summed = None
    own_rows = None
    weight_grad = jnp.einsum("nd,lnc->ldc", columns, block, preferred_element_type=jnp.float32)
    own_rows = lax.all_to_all(row_terms, "dp", split_axis=0, concat_axis=1, tiled=True)
    summed = lax.psum_scatter(own_rows, "layer", scatter_dimension=1, tiled=True)
    return (summed.astype(jnp.bfloat16), weight_grad.astype(jnp.bfloat16))


def solution(mesh):
    return jax.shard_map(
        local,
        mesh=mesh,
        in_specs=(
            P("dp", None),
            P("layer", "dp", None),
            P("layer", "dp", None),
            P("layer", "dp", None),
            P("layer", "dp", None),
            P("layer", "dp", None),
            P("dp", None),
        ),
        out_specs=(P("dp", "layer"), P("layer", "dp", None)),
        check_vma=False,
    )
```

profile of v0, /device:TPU:19, one launch (start us, length us, event | category | flops | bytes accessed | tf_op | source)
XLA Modules:
  0.0 383.7 jit_solution(5285715884629875186)
XLA Ops:
  7.2 0.9 reduce-window.8
  8.4 0.9 reshape_squeeze.14
  9.3 0.9 reshape_squeeze.12
  10.2 2.3 copy.87
  12.8 1.7 copy.70
  14.5 2.2 fusion.40
  16.7 1.8 fusion.22
  18.5 1.7 copy.64
  20.2 1.7 fusion.17
  22.0 0.9 fusion.3
  23.2 2.6 fusion.16
  26.6 89.5 %all-gather.2.cloned.1.call-done = bf16[1,4096,1024]{1,2,0:T(8,128)(2,1)} async-done(((bf16[1,128,1024]{1,2,0:T(8,128)(2,1)}), bf16[1,4096,1024]{1,2,0:T(8,128)(2,1)}) %all-gather.2.cloned.1.call-update) | async-done | bytes 8388624 | tf_op jit(solution)/shard_map/all_gather | solution.py:64
  116.1 11.9 %copy.71 = bf16[1,4096,1024]{2,1,0:T(8,128)(2,1)} copy(bf16[1,4096,1024]{1,2,0:T(8,128)(2,1)} %all-gather.2.cloned.1.call-done) | data formatting | bytes 16777216 | tf_op jit(solution)/shard_map/all_gather | solution.py:64
  128.0 5.8 %fusion.23 = f32[32,128,256]{2,1,0:T(8,128)S(1)} fusion(bf16[32,128,1024]{2,1,0:T(8,128)(2,1)} %bitcast.89, bf16[1,256,1024]{2,1,0:T(8,128)(2,1)S(1)} %copy-done), kind=kOutput, calls=%fused_computation.25 | convolution fusion | flops 2147483648 | bytes 13107200 | tf_op jit(solution)/shard_map/lnc,ldc->nd/dot_general | solution.py:65
  133.8 100.5 %all_to_all.35 = f32[32,128,256]{2,1,0:T(8,128)} all-to-all(f32[32,128,256]{2,1,0:T(8,128)S(1)} %fusion.23), channel_id=1, replica_groups=mesh['dp'=32,'layer'=8] {'dp'}, dimensions={0} | all-to-all | bytes 8388608 | tf_op jit(solution)/shard_map/all_to_all | solution.py:69
  234.3 5.6 %copy.72 = f32[128,32,256]{0,2,1:T(8,128)} copy(f32[128,32,256]{2,0,1:T(8,128)} %bitcast.86) | data formatting | bytes 8388608 | tf_op jit(solution)/shard_map/all_to_all | solution.py:69
  239.9 1.6 copy-done.3
  241.5 2.5 copy.73
  243.9 99.4 %all_to_all.36 = bf16[128,32,256]{0,2,1:T(8,128)(2,1)S(1)} all-to-all(bf16[128,32,256]{0,2,1:T(8,128)(2,1)} %bitcast.91), channel_id=1, replica_groups=mesh['dp'=32,'layer'=8] {'dp'}, dimensions={1} | all-to-all | bytes 4194304 | tf_op jit(solution)/shard_map/all_to_all | solution.py:63
  343.3 2.9 copy.74
  346.2 6.3 %fusion.11 = bf16[1,256,1024]{1,2,0:T(8,128)(2,1)S(1)} fusion(bf16[4096,256]{1,0:T(8,128)(2,1)} %bitcast.92, bf16[1,4096,1024]{1,2,0:T(8,128)(2,1)} %all-gather.2.cloned.1.call-done), kind=kOutput, calls=%fused_computation.13 | convolution fusion | flops 2147745792 | bytes 11010048 | tf_op jit(solution)/shard_map/nd,lnc->ldc/dot_general | solution.py:68
  352.5 1.0 copy.76
  353.5 21.4 %reduce-scatter.2.cloned.1.call-done = f32[128,1024]{0,1:T(8,128)} async-done(((f32[128,8192]{0,1:T(8,128)}), f32[128,1024]{0,1:T(8,128)}) %reduce-scatter.2.cloned.1.call-update) | async-done | bytes 524304 | tf_op jit(solution)/shard_map/reduce_scatter | solution.py:70
  374.9 1.1 convert_element_type.36
  (21 shorter events, 2.4 us)
Async XLA Ops:
  7.2 120.9 %copy-start = (bf16[1,256,1024]{2,1,0:T(8,128)(2,1)S(1)}, bf16[1,256,1024]{2,1,0:T(8,128)(2,1)}, u32[]{:S(2)}) copy-start(bf16[1,256,1024]{2,1,0:T(8,128)(2,1)} %param.8) | copy-start | bytes 1572868
  7.2 5.3 %copy-start.4 = (bf16[1,128,4096]{2,1,0:T(8,128)(2,1)S(1)}, bf16[1,128,4096]{2,1,0:T(8,128)(2,1)}, u32[]{:S(2)}) copy-start(bf16[1,128,4096]{2,1,0:T(8,128)(2,1)} %param.12) | copy-start | bytes 3145732
  7.2 108.9 %all-gather.2.cloned.1.call-start = ((), (), s32[]{:S(2)}) async-start(), calls=%async_computation.3 | async-start | bytes 8650752 | tf_op jit(solution)/shard_map/all_gather | solution.py:64
  12.8 1.7 copy-start.5
  20.2 1.8 copy-start.2
  22.0 1.2 copy-start.1
  26.6 348.3 %reduce-scatter.2.cloned.1.call-start = ((), (), s32[]{:S(2)}) async-start(), calls=%async_computation.4 | async-start | bytes 4718592 | tf_op jit(solution)/shard_map/reduce_scatter | solution.py:70
  239.9 1.6 copy-start.3
Sparse Core Ops, SparseCore 0:
  26.7 89.3 all-gather.1
  240.0 134.8 reduce-scatter.1
where the time goes:
time: 387 us; the launch traced here: 384 us
  blocking collectives  200 us (52%)
  waiting for transfers between devices  111 us (29%)
  local copies, waits for them, and re-layouts  34.4 us (9%)
  matrix products  19.5 us (5%)
  between operations  14.2 us (4%)
  other arithmetic  4.75 us (1%)
    all_to_all x1, blocking collectives, local(): lax.all_to_all(row_terms, 'dp', split_axis=0, concat_axis=1, tiled=True)  100 us
    all_to_all x1, blocking collectives, local(): lax.all_to_all(hidden, 'dp', split_axis=1, concat_axis=0, tiled=True)  99.4 us
    all_gather x1, waiting for transfers between devices, local(): block = lax.all_gather(key_value_gradient, 'dp', axis=1, tiled=True)  89.5 us
    reduce_scatter x1, waiting for transfers between devices, local(): lax.psum_scatter(own_rows, 'layer', scatter_dimension=1, tiled=True)  21.4 us
    all_gather x1, local copies, waits for them, and re-layouts, local(): block = lax.all_gather(key_value_gradient, 'dp', axis=1, tiled=True)  11.9 us
  transfers between devices with their start and end apart: 2, of which 2 were waited for; matrix products, arithmetic and copies ran while one was open for 3% of the time, Pallas kernels for 0%

commit v1 on v0

v1 whole, which is shorter than its diff:
```python
import jax
import jax.numpy as jnp
from jax import lax
from jax.experimental import pallas as pl
from jax.experimental.pallas import tpu as pltpu
from jax.sharding import PartitionSpec as P

HEAD = 128
GROUPS = 4
PER = 8
TOK = 128
DOCS = 8
KV = 512
KV2 = 1024
SCALE = HEAD ** (-0.5)
MESH = pl.DeviceIdType.MESH
NT = (((1,), (1,)), ((), ()))


def xor(a, b):
    return jnp.bitwise_xor(a, b)


def body(lens, hidden, w, q, k, v, dout, gh, gw,
         hid, hid_t, wb, kvb, st, rs, own, gsend, grecv, fs, fin,
         hz_s, hz_r, hc_s, hc_r, hx_s, hx_r, w_s, w_r, kz_s, kz_r, kf_s, kf_r,
         x_s, x_r, g_s, g_r, f_s, f_r, loc):
    dp, ly = lax.axis_index("dp"), lax.axis_index("layer")
    y, z, c = dp // 8, lax.rem(dp // 2, 4), lax.rem(dp, 2)
    h, x = ly // 4, lax.rem(ly, 4)
    y0, y1, z0, z1, x0, x1 = lax.rem(y, 2), y // 2, lax.rem(z, 2), z // 2, lax.rem(x, 2), x // 2

    def dev(yy, zz, cc, hh, xx):
        return ((yy * 4 + zz) * 2 + cc, hh * 4 + xx)

    def send(src, dst, s, r, to):
        return pltpu.make_async_remote_copy(src_ref=src, dst_ref=dst, send_sem=s, recv_sem=r,
                                            device_id=to, device_id_type=MESH)

    a_own, b_own = xor(x1, y0), xor(x0, z1)
    aligned = x0 == z1
    xt = 2 * x1 + z1

    def last(i, i2, j):
        return dev(y, 2 * x0 + xor(z0, i), xor(c, j), xor(y1, i2), xt)

    sib = dev(y, z, 1 - c, h, x)
    zdev = [None] + [dev(y, xor(z, kk), c, h, x) for kk in (1, 2, 3)]
    zsib = [None] + [dev(y, xor(z, kk), 1 - c, h, x) for kk in (1, 2, 3)]
    xdev = [None] + [dev(y, z, c, h, xor(x, qq)) for qq in (1, 2, 3)]
    ydev = [None] + [dev(xor(y, r), z, c, h, x) for r in (1, 2, 3)]

    barrier = pltpu.get_barrier_semaphore()
    for to in [sib] + zdev[1:] + zsib[1:] + xdev[1:] + ydev[1:]:
        pl.semaphore_signal(barrier, inc=1, device_id=to, device_id_type=MESH)
    for i in range(2):
        for i2 in range(2):
            for j in range(2):
                to = last(i, i2, j)
                if i == 0 and j == 0:
                    me = jnp.logical_and(aligned, xor(y1, i2) == h)

                    @pl.when(jnp.logical_not(me))
                    def _():
                        pl.semaphore_signal(barrier, inc=1, device_id=to, device_id_type=MESH)
                else:
                    pl.semaphore_signal(barrier, inc=1, device_id=to, device_id_type=MESH)

    def columns(p, zz, cc):
        return pl.ds(pl.multiple_of(p * 2048 + zz * 512 + cc * 256, 256), 256)

    local = [pltpu.make_async_copy(w.at[0], wb.at[0], loc.at[0])]
    for r in range(4):
        local.append(pltpu.make_async_copy(hidden.at[:, columns(xor(y, r), z, c)],
                                           hid.at[r, pl.ds(0, TOK)], loc.at[1 + r]))
    for cp in local:
        cp.start()

    pl.semaphore_wait(barrier, 20 + jnp.where(aligned, 0, 1))

    hz = []
    for kk in (1, 2, 3):
        for j in range(2):
            rows = pl.ds(kk * 256 + j * TOK, TOK)
            hz.append(send(hidden.at[:, columns(xor(y, x), xor(z, kk), xor(c, j))],
                           hid.at[x, rows], hz_s.at[kk, j], hz_r.at[kk, j], (zsib if j else zdev)[kk]))
    wc = [send(w.at[0], wb.at[r], w_s.at[r], w_r.at[r], ydev[r]) for r in (1, 3, 2)]
    hc = [send(hidden.at[:, columns(xor(y, r), z, 1 - c)], hid.at[r, pl.ds(TOK, TOK)],
               hc_s.at[r], hc_r.at[r], sib) for r in range(4)]
    for cp in hz + wc + hc:
        cp.start()

    row = lax.broadcasted_iota(jnp.int32, (TOK, TOK), 0)
    col = lax.broadcasted_iota(jnp.int32, (TOK, TOK), 1)
    doc_row, doc_col = jnp.zeros_like(row), jnp.zeros_like(col)
    end = jnp.int32(0)
    for d in range(DOCS):
        end = end + lens[0, d]
        doc_row = doc_row + jnp.where(row >= end, 1, 0)
        doc_col = doc_col + jnp.where(col >= end, 1, 0)
    bias = jnp.where((doc_row == doc_col) & (row <= col), 0.0, 1.0)
    off = jnp.concatenate([bias] * PER, axis=1) > 0.5

    def group(g, _):
        wide = pl.multiple_of(g * PER * HEAD, PER * HEAD)
        narrow = pl.multiple_of(g * HEAD, HEAD)
        qg, og = q[0, :, pl.ds(wide, PER * HEAD)], dout[0, :, pl.ds(wide, PER * HEAD)]
        qs = jnp.concatenate([qg[:, n * HEAD:(n + 1) * HEAD] for n in range(PER)], axis=0)
        os = jnp.concatenate([og[:, n * HEAD:(n + 1) * HEAD] for n in range(PER)], axis=0)
        kg, vg = k[0, :, pl.ds(narrow, HEAD)], v[0, :, pl.ds(narrow, HEAD)]
        s = lax.dot_general(kg, qs, NT, preferred_element_type=jnp.float32) * SCALE
        s = jnp.where(off, jnp.float32(-1e30), s)
        e = jnp.exp(s - jnp.max(s, axis=0, keepdims=True))
        p = e / jnp.sum(e, axis=0, keepdims=True)
        pb = p.astype(jnp.bfloat16)
        dp_ = lax.dot_general(vg, os, NT, preferred_element_type=jnp.float32)
        delta = jnp.sum(pb.astype(jnp.float32) * dp_, axis=0, keepdims=True)
        ds = (p * (dp_ - delta)).astype(jnp.bfloat16)
        dv = jnp.dot(pb, os, preferred_element_type=jnp.float32)
        dk = jnp.dot(ds, qs, preferred_element_type=jnp.float32) * SCALE
        kvb[0:TOK, pl.ds(narrow, HEAD)] = dk.astype(jnp.bfloat16)
        kvb[0:TOK, pl.ds(pl.multiple_of(KV + g * HEAD, HEAD), HEAD)] = dv.astype(jnp.bfloat16)
        return 0

    lax.fori_loop(0, GROUPS, group, 0)

    def kv_rows(kk, j):
        return pl.ds(kk * 256 + j * TOK, TOK)

    kz = {kk: send(kvb.at[kv_rows(0, 0)], kvb.at[kv_rows(kk, 0)], kz_s.at[kk], kz_r.at[kk], zdev[kk])
          for kk in (1, 2, 3)}
    kf = {kk: send(kvb.at[kv_rows(kk, 0)], kvb.at[kv_rows(kk, 1)], kf_s.at[kk], kf_r.at[kk], sib)
          for kk in range(4)}
    kf[0].start()
    for kk in (1, 2, 3):
        kz[kk].start()

    for cp in hz:
        cp.wait_recv()
    rest = pl.ds(256, 768)
    hx = [send(hid.at[x, rest], hid.at[x, rest], hx_s.at[qq], hx_r.at[qq], xdev[qq]) for qq in (1, 3, 2)]
    for cp in hx:
        cp.start()
    for cp in local:
        cp.wait()

    def tile(kk, r):
        t = lax.dot_general(kvb[kk * 256:(kk + 1) * 256], wb[r], NT, preferred_element_type=jnp.float32)
        st[kk, r] = t.astype(jnp.bfloat16)
        to_x = 2 * xor(y0, r % 2) + xor(z1, kk // 2)
        qq = xor(to_x, x)

        @pl.when(qq != 0)
        def _():
            send(st.at[kk, r], rs.at[qq, kk % 2, r // 2], x_s.at[kk, r], x_r.at[qq, kk % 2, r // 2],
                 dev(y, z, c, h, to_x)).start()

    for kk in range(4):
        if kk:
            kz[kk].wait_recv()
            kf[kk].start()
        kf[kk].wait_recv()
        for n, r in enumerate((0, 1, 3, 2)):
            if kk == 0 and n:
                wc[n - 1].wait_recv()
            tile(kk, r)

    for cp in hx + hc:
        cp.wait_recv()
    for r in range(4):
        hid_t[r] = hid[r].T
    gc = []
    for r in (2, 1, 3, 0):
        t = jnp.dot(hid_t[r], kvb[...], preferred_element_type=jnp.float32)
        if r:
            gsend[r - 1] = t.astype(jnp.bfloat16)
            cp = send(gsend.at[r - 1], grecv.at[r - 1], g_s.at[r], g_r.at[r], ydev[r])
            cp.start()
            gc.append(cp)
        else:
            own[...] = t

    for i in range(2):
        for i2 in range(2):
            for qq in (1, 2, 3):
                send(rs.at[qq, i, i2], rs.at[qq, i, i2], x_s.at[0, 0], x_r.at[qq, i, i2], xdev[qq]).wait_recv()
            t = st[2 * b_own + i, a_own + 2 * i2].astype(jnp.float32)
            for qq in (1, 2, 3):
                t = t + rs[qq, i, i2].astype(jnp.float32)
            fs[i, i2] = t.astype(jnp.bfloat16)
            ht = xor(y1, i2)
            g = xor(ht, h)
            for j in range(2):
                src = fs.at[i, i2, pl.ds(j * TOK, TOK)]
                to = last(i, i2, j)
                if i == 0 and j == 0:
                    me = jnp.logical_and(aligned, g == 0)

                    @pl.when(me)
                    def _():
                        pltpu.make_async_copy(src, fin.at[g, i, j], f_r.at[g, i, j]).start()

                    @pl.when(jnp.logical_not(me))
                    def _():
                        send(src, fin.at[g, i, j], f_s.at[i, i2, j], f_r.at[g, i, j], to).start()
                else:
                    send(src, fin.at[g, i, j], f_s.at[i, i2, j], f_r.at[g, i, j], to).start()

    for i in range(2):
        for j in range(2):
            for g in range(2):
                send(fin.at[g, i, j], fin.at[g, i, j], f_s.at[0, 0, 0], f_r.at[g, i, j], sib).wait_recv()
            t = fin[0, i, j].astype(jnp.float32) + fin[1, i, j].astype(jnp.float32)
            gh[:, pl.ds(pl.multiple_of(xor(z0, i) * 512 + xor(c, j) * 256, 256), 256)] = t.astype(jnp.bfloat16)

    for cp in gc:
        cp.wait_recv()
    t = own[...]
    for r in range(3):
        t = t + grecv[r].astype(jnp.float32)
    gw[0] = t.astype(jnp.bfloat16)

    for cp in hz + wc + hc + hx + gc:
        cp.wait_send()
    for kk in (1, 2, 3):
        kz[kk].wait_send()
    for kk in range(4):
        kf[kk].wait_send()
    for kk in range(4):
        for r in range(4):
            qq = xor(2 * xor(y0, r % 2) + xor(z1, kk // 2), x)

            @pl.when(qq != 0)
            def _():
                send(st.at[kk, r], st.at[kk, r], x_s.at[kk, r], x_r.at[0, 0, 0], sib).wait_send()
    for i in range(2):
        for i2 in range(2):
            for j in range(2):
                cp = send(fs.at[i, i2, pl.ds(j * TOK, TOK)], fin.at[0, 0, 0], f_s.at[i, i2, j], f_r.at[0, 0, 0], sib)
                if i == 0 and j == 0:
                    me = jnp.logical_and(aligned, xor(y1, i2) == h)

                    @pl.when(jnp.logical_not(me))
                    def _():
                        cp.wait_send()
                else:
                    cp.wait_send()


def local(hidden, w_kv, queries, keys, values, out_grad, doc_lengths):
    bf, f32, dma = jnp.bfloat16, jnp.float32, pltpu.SemaphoreType.DMA
    vm, hbm = pl.BlockSpec(memory_space=pltpu.VMEM), pl.BlockSpec(memory_space=pl.ANY)
    return pl.pallas_call(
        body,
        out_shape=(jax.ShapeDtypeStruct((TOK, 1024), bf), jax.ShapeDtypeStruct((1, 256, KV2), bf)),
        in_specs=[pl.BlockSpec(memory_space=pltpu.SMEM), hbm, hbm, vm, vm, vm, vm],
        out_specs=(vm, vm),
        scratch_shapes=[
            pltpu.VMEM((4, 1024, 256), bf),
            pltpu.VMEM((4, 256, 1024), bf),
            pltpu.VMEM((4, 256, KV2), bf),
            pltpu.VMEM((1024, KV2), bf),
            pltpu.VMEM((4, 4, 256, 256), bf),
            pltpu.VMEM((4, 2, 2, 256, 256), bf),
            pltpu.VMEM((256, KV2), f32),
            pltpu.VMEM((3, 256, KV2), bf),
            pltpu.VMEM((3, 256, KV2), bf),
            pltpu.VMEM((2, 2, 256, 256), bf),
            pltpu.VMEM((2, 2, 2, TOK, 256), bf),
            dma((4, 2)), dma((4, 2)), dma((4,)), dma((4,)), dma((4,)), dma((4,)), dma((4,)), dma((4,)),
            dma((4,)), dma((4,)), dma((4,)), dma((4,)),
            dma((4, 4)), dma((4, 2, 2)), dma((4,)), dma((4,)), dma((2, 2, 2)), dma((2, 2, 2)), dma((5,)),
        ],
        compiler_params=pltpu.CompilerParams(
            collective_id=0, has_side_effects=True, vmem_limit_bytes=48 * 2**20),
        cost_estimate=pl.CostEstimate(flops=5 * 10**9, bytes_accessed=8 * 2**20, transcendentals=2**19),
    )(doc_lengths, hidden, w_kv, queries, keys, values, out_grad)


def solution(mesh):
    return jax.shard_map(
        local,
        mesh=mesh,
        in_specs=(
            P("dp", None),
            P("layer", "dp", None),
            P("layer", "dp", None),
            P("layer", "dp", None),
            P("layer", "dp", None),
            P("layer", "dp", None),
            P("dp", None),
        ),
        out_specs=(P("dp", "layer"), P("layer", "dp", None)),
        check_vma=False,
    )
```

time: 387 us -> 88.5 us (0.23)
  blocking collectives: 200 us -> 0 us
  waiting for transfers between devices: 111 us -> 0 us
  Pallas kernels: 0 us -> 78.5 us
  local copies, waits for them, and re-layouts: 34.4 us -> 9.03 us
  matrix products: 19.5 us -> 0 us
  between operations: 14.2 us -> 0.66 us
  other arithmetic: 4.75 us -> 0 us
    all_to_all x2 -> x0, blocking collectives: 200 us -> none  [the longest x1 100 us: local(): lax.all_to_all(row_terms, 'dp', split_axis=0, concat_axis=1, tiled=True)]
    all_gather x1 -> x0, waiting for transfers between devices: 89.5 us -> none  [local(): block = lax.all_gather(key_value_gradient, 'dp', axis=1, tiled=True)]
    pallas_call x0 -> x1, Pallas kernels: none -> 78.5 us  [local(): pl.pallas_call(body, out_shape=(jax.ShapeDtypeStruct((TOK, 1024), bf), ja...]
    reduce_scatter x1 -> x0, waiting for transfers between devices: 21.4 us -> none  [local(): lax.psum_scatter(own_rows, 'layer', scatter_dimension=1, tiled=True)]
    dot_general x5 -> x0, matrix products: 17.3 us -> none  [the longest x1 6.3 us: local(): jnp.einsum('nd,lnc->ldc', columns, block, preferred_element_type=jnp.floa...]
    all_gather x1 -> x0, local copies, waits for them, and re-layouts: 11.9 us -> none  [local(): block = lax.all_gather(key_value_gradient, 'dp', axis=1, tiled=True)]
    all_to_all x2 -> x0, local copies, waits for them, and re-layouts: 8.48 us -> none  [the longest x1 5.56 us: local(): lax.all_to_all(row_terms, 'dp', split_axis=0, concat_axis=1, tiled=True)]
    another operation x4 -> x0, local copies, waits for them, and re-layouts: 5.88 us -> none  [the longest x1 2.28 us: attend_back(): query_block_tile.reshape(element_count, KV_HEAD_COUNT, QUERY_PER_KV, HEAD...]
  transfers between devices with their start and end apart: 2 -> 0, of which waited for: 2 -> 0; matrix products, arithmetic and copies ran while one was open for 3% -> 0% of each run, Pallas kernels for 0% -> 0%
where the time goes in v1:
time: 88.5 us; the launch traced here: 88.2 us
  Pallas kernels  78.5 us (89%)
  local copies, waits for them, and re-layouts  9.03 us (10%)
    pallas_call x1, Pallas kernels, local(): pl.pallas_call(body, out_shape=(jax.ShapeDtypeStruct((TOK, 1024), bf), ja...  78.5 us
    unnamed x16, local copies, waits for them, and re-layouts  9.03 us

profile of v1, /device:TPU:19, one launch (start us, length us, event | category | flops | bytes accessed | tf_op | source)
XLA Modules:
  0.0 88.2 jit_solution(394130621113048465)
XLA Ops:
  0.6 0.0 copy-start
  0.6 1.6 %copy-done = bf16[128,8192]{1,0:T(8,128)(2,1)S(1)} copy-done((bf16[128,8192]{1,0:T(8,128)(2,1)S(1)}, bf16[128,8192]{1,0:T(8,128)(2,1)}, u32[]{:S(2)}) %copy-start) | copy-done | bytes 2097176
  2.2 0.0 copy-start.1
  2.2 1.2 %copy-done.1 = bf16[1,128,4096]{2,1,0:T(8,128)(2,1)S(1)} copy-done((bf16[1,128,4096]{2,1,0:T(8,128)(2,1)S(1)}, bf16[1,128,4096]{2,1,0:T(8,128)(2,1)}, u32[]{:S(2)}) %copy-start.1) | copy-done | bytes 1048600
  3.4 0.0 copy-start.2
  3.5 1.2 %copy-done.2 = bf16[1,128,4096]{2,1,0:T(8,128)(2,1)S(1)} copy-done((bf16[1,128,4096]{2,1,0:T(8,128)(2,1)S(1)}, bf16[1,128,4096]{2,1,0:T(8,128)(2,1)}, u32[]{:S(2)}) %copy-start.2) | copy-done | bytes 1048600
  4.7 0.0 copy-start.3
  4.7 1.0 %copy-done.3 = bf16[1,256,1024]{2,1,0:T(8,128)(2,1)S(1)} copy-done((bf16[1,256,1024]{2,1,0:T(8,128)(2,1)S(1)}, bf16[1,256,1024]{2,1,0:T(8,128)(2,1)}, u32[]{:S(2)}) %copy-start.3) | copy-done | bytes 524312
  5.7 0.0 copy-start.4
  5.7 0.9 %copy-done.4 = bf16[1,128,512]{2,1,0:T(8,128)(2,1)S(1)} copy-done((bf16[1,128,512]{2,1,0:T(8,128)(2,1)S(1)}, bf16[1,128,512]{2,1,0:T(8,128)(2,1)}, u32[]{:S(2)}) %copy-start.4) | copy-done | bytes 131096
  6.6 0.0 copy-start.5
  6.6 0.9 %copy-done.5 = bf16[1,128,512]{2,1,0:T(8,128)(2,1)S(1)} copy-done((bf16[1,128,512]{2,1,0:T(8,128)(2,1)S(1)}, bf16[1,128,512]{2,1,0:T(8,128)(2,1)}, u32[]{:S(2)}) %copy-start.5) | copy-done | bytes 131096
  7.5 0.0 copy-start.6
  7.5 0.7 copy-done.6
  8.2 78.5 %shard_map.86 = (bf16[128,1024]{1,0:T(8,128)(2,1)S(1)}, bf16[1,256,1024]{2,1,0:T(8,128)(2,1)S(1)}) custom-call(s32[1,8]{1,0:T(1,128)S(1)} %copy-done.6, bf16[128,8192]{1,0:T(8,128)(2,1)S(1)} %copy-done, bf16[1,256,1024]{2,1,0:T(8,128)(2,1)S(1)} %copy-done.3, bf16[1,128,4096]{2,1,0:T(8,128)(2,1)S(1)} %copy-done.1, bf16[1,128,512]{2,1,0:T(8,128)(2,1)S(1)} %copy-done.4, ...), custom_call_target="tpu_custom_call" | custom-call | flops 5000000000 | bytes 8388608 | tf_op jit(solution)/shard_map/pallas_call | solution.py:253
  86.7 0.7 copy.11
  87.4 0.8 copy.12
Async XLA Ops:
  0.6 1.6 %copy-start = (bf16[128,8192]{1,0:T(8,128)(2,1)S(1)}, bf16[128,8192]{1,0:T(8,128)(2,1)}, u32[]{:S(2)}) copy-start(bf16[128,8192]{1,0:T(8,128)(2,1)} %hidden.1) | copy-start | bytes 6291460
  2.2 1.2 %copy-start.1 = (bf16[1,128,4096]{2,1,0:T(8,128)(2,1)S(1)}, bf16[1,128,4096]{2,1,0:T(8,128)(2,1)}, u32[]{:S(2)}) copy-start(bf16[1,128,4096]{2,1,0:T(8,128)(2,1)} %q.1) | copy-start | bytes 3145732
  3.4 1.2 %copy-start.2 = (bf16[1,128,4096]{2,1,0:T(8,128)(2,1)S(1)}, bf16[1,128,4096]{2,1,0:T(8,128)(2,1)}, u32[]{:S(2)}) copy-start(bf16[1,128,4096]{2,1,0:T(8,128)(2,1)} %dout.1) | copy-start | bytes 3145732
  4.7 1.0 %copy-start.3 = (bf16[1,256,1024]{2,1,0:T(8,128)(2,1)S(1)}, bf16[1,256,1024]{2,1,0:T(8,128)(2,1)}, u32[]{:S(2)}) copy-start(bf16[1,256,1024]{2,1,0:T(8,128)(2,1)} %w.1) | copy-start | bytes 1572868
  5.7 0.9 %copy-start.4 = (bf16[1,128,512]{2,1,0:T(8,128)(2,1)S(1)}, bf16[1,128,512]{2,1,0:T(8,128)(2,1)}, u32[]{:S(2)}) copy-start(bf16[1,128,512]{2,1,0:T(8,128)(2,1)} %k.1) | copy-start | bytes 393220
  6.6 0.9 %copy-start.5 = (bf16[1,128,512]{2,1,0:T(8,128)(2,1)S(1)}, bf16[1,128,512]{2,1,0:T(8,128)(2,1)}, u32[]{:S(2)}) copy-start(bf16[1,128,512]{2,1,0:T(8,128)(2,1)} %v.1) | copy-start | bytes 393220
  7.5 0.7 copy-start.6

commit v2 on v1

v2 whole, which is shorter than its diff:
```python
import jax
import jax.numpy as jnp
from jax import lax
from jax.experimental import pallas as pl
from jax.experimental.pallas import tpu as pltpu
from jax.sharding import PartitionSpec as P

HEAD = 128
GROUPS = 4
PER = 8
TOK = 128
DOCS = 8
KV = 512
KV2 = 1024
SCALE = HEAD ** (-0.5)
MESH = pl.DeviceIdType.MESH
NT = (((1,), (1,)), ((), ()))
HALF = (pl.ds(0, 128), pl.ds(128, 128))
PART = (pl.ds(256, 384), pl.ds(640, 384))


def xor(a, b):
    return jnp.bitwise_xor(a, b)


def body(lens_in, hidden, w, q_in, k_in, v_in, dout_in, gh, gw,
         lens, q, k, v, dout,
         hsrc, hid, hid_t, wb, kvb, st, rs, own, keep, gs2, gr2, gsend, grecv, fs, fin,
         hz_s, hz_r, hc_s, hc_r, hx_s, hx_r, w_s, w_r, kz_s, kz_r, kf_s, kf_r,
         x_s, x_r, g_s, g_r, g2_s, g2_r, f_s, f_r, loc):
    dp, ly = lax.axis_index("dp"), lax.axis_index("layer")
    y, z, c = dp // 8, lax.rem(dp // 2, 4), lax.rem(dp, 2)
    h, x = ly // 4, lax.rem(ly, 4)
    y0, y1, z0, z1, x0, x1 = lax.rem(y, 2), y // 2, lax.rem(z, 2), z // 2, lax.rem(x, 2), x // 2

    def dev(yy, zz, cc, hh, xx):
        return ((yy * 4 + zz) * 2 + cc, hh * 4 + xx)

    def ring(d, cc):
        p = lax.rem(h * 4 + z + d + 8, 8)
        return dev(y, lax.rem(p, 4), cc, p // 4, x)

    def send(src, dst, s, r, to):
        return pltpu.make_async_remote_copy(src_ref=src, dst_ref=dst, send_sem=s, recv_sem=r,
                                            device_id=to, device_id_type=MESH)

    def signal(to):
        pl.semaphore_signal(barrier, inc=1, device_id=to, device_id_type=MESH)

    ta, tb = xor(x1, y0), xor(x0, z1)
    aligned = tb == 0
    middle = z0 != z1
    xt = 2 * x1 + z1

    def last(i, i2, j):
        return dev(y, 2 * x0 + xor(z0, i), xor(c, j), xor(y1, i2), xt)

    sib = dev(y, z, 1 - c, h, x)
    zdev = {kk: dev(y, xor(z, kk), c, h, x) for kk in (1, 3)}
    xdev = {qq: dev(y, z, c, h, xor(x, qq)) for qq in (1, 2, 3)}
    ydev = {r: dev(xor(y, r), z, c, h, x) for r in (1, 3)}

    barrier = pltpu.get_barrier_semaphore()
    for to in [sib, zdev[1], xdev[1], xdev[2], xdev[3], ydev[1], ydev[3],
               ring(1, 0), ring(1, 1), ring(-1, 0), ring(-1, 1), ring(-2, 0), ring(2, 1)]:
        signal(to)

    @pl.when(middle)
    def _():
        signal(zdev[3])

    for i in range(2):
        for i2 in range(2):
            for j in range(2):
                to = last(i, i2, j)
                if i == 0 and j == 0:
                    @pl.when(jnp.logical_not(jnp.logical_and(aligned, xor(y1, i2) == h)))
                    def _():
                        signal(to)
                else:
                    signal(to)

    def columns(p, zz, cc):
        return pl.ds(pl.multiple_of(p * 2048 + zz * 512 + cc * 256, 256), 256)

    loads = [pltpu.make_async_copy(lens_in, lens, loc.at[0])]
    for n, (src, dst) in enumerate(((k_in, k), (q_in, q), (v_in, v), (dout_in, dout))):
        loads.append(pltpu.make_async_copy(src.at[0], dst, loc.at[1 + n]))
    for r in range(4):
        loads.append(pltpu.make_async_copy(hidden.at[:, columns(xor(y, r), z, c)],
                                           hid.at[r, pl.ds(0, TOK)], loc.at[5 + r]))
    loads.append(pltpu.make_async_copy(w.at[0], wb.at[0], loc.at[9]))
    steps = (1, -1, 2 - 4 * c)
    first = [pltpu.make_async_copy(hidden.at[:, columns(xor(y, x), lax.rem(z + d + 4, 4), xor(c, j))],
                                   hsrc.at[n, j], loc.at[10 + 2 * n + j])
             for n, d in enumerate(steps) for j in range(2)]
    for cp in first + loads[9:] + loads[:9]:
        cp.start()
    for cp in first + loads[9:]:
        cp.wait()

    pl.semaphore_wait(barrier, 20 + jnp.where(middle, 1, 0) + jnp.where(aligned, 0, 1))

    hz = []
    for n, d in enumerate(steps):
        zt = lax.rem(z + d + 4, 4)
        for j in range(2):
            cc = xor(c, j)
            rows = pl.ds(pl.multiple_of(xor(z, zt) * 256 + j * TOK, TOK), TOK)
            hz.append(send(hsrc.at[n, j], hid.at[x, rows], hz_s.at[n, j], hz_r.at[n, j], ring(d, cc)))
    wc = {(r, n): send(wb.at[0, HALF[n]], wb.at[r, HALF[n]], w_s.at[r - 1, n], w_r.at[r - 1, n], ydev[r])
          for r, n in ((1, 0), (3, 1), (1, 1), (3, 0))}
    wc[2, 0] = send(wb.at[1, HALF[0]], wb.at[2, HALF[0]], w_s.at[1, 0], w_r.at[1, 0], ydev[3])
    wc[2, 1] = send(wb.at[3, HALF[1]], wb.at[2, HALF[1]], w_s.at[1, 1], w_r.at[1, 1], ydev[1])
    hc = [send(hidden.at[:, columns(xor(y, r), z, 1 - c)], hid.at[r, pl.ds(TOK, TOK)],
               hc_s.at[r], hc_r.at[r], sib) for r in range(4)]
    for cp in hz:
        cp.start()
    for key in ((1, 0), (3, 1)):
        wc[key].start()
    for cp in hc:
        cp.start()

    loads[0].wait()
    row = lax.broadcasted_iota(jnp.int32, (TOK, TOK), 0)
    col = lax.broadcasted_iota(jnp.int32, (TOK, TOK), 1)
    doc_row, doc_col = jnp.zeros_like(row), jnp.zeros_like(col)
    end = jnp.int32(0)
    for d in range(DOCS):
        end = end + lens[0, d]
        doc_row = doc_row + jnp.where(row >= end, 1, 0)
        doc_col = doc_col + jnp.where(col >= end, 1, 0)
    bias = jnp.where((doc_row == doc_col) & (row <= col), 0.0, 1.0)
    off = jnp.concatenate([bias] * PER, axis=1) > 0.5
    for cp in loads[1:5]:
        cp.wait()

    def group(g, _):
        wide = pl.multiple_of(g * PER * HEAD, PER * HEAD)
        narrow = pl.multiple_of(g * HEAD, HEAD)
        qg, og = q[:, pl.ds(wide, PER * HEAD)], dout[:, pl.ds(wide, PER * HEAD)]
        qs = jnp.concatenate([qg[:, n * HEAD:(n + 1) * HEAD] for n in range(PER)], axis=0)
        os = jnp.concatenate([og[:, n * HEAD:(n + 1) * HEAD] for n in range(PER)], axis=0)
        kg, vg = k[:, pl.ds(narrow, HEAD)], v[:, pl.ds(narrow, HEAD)]
        s = lax.dot_general(kg, qs, NT, preferred_element_type=jnp.float32) * SCALE
        s = jnp.where(off, jnp.float32(-1e30), s)
        e = jnp.exp(s - jnp.max(s, axis=0, keepdims=True))
        p = e / jnp.sum(e, axis=0, keepdims=True)
        pb = p.astype(jnp.bfloat16)
        dp_ = lax.dot_general(vg, os, NT, preferred_element_type=jnp.float32)
        delta = jnp.sum(pb.astype(jnp.float32) * dp_, axis=0, keepdims=True)
        ds = (p * (dp_ - delta)).astype(jnp.bfloat16)
        dv = jnp.dot(pb, os, preferred_element_type=jnp.float32)
        dk = jnp.dot(ds, qs, preferred_element_type=jnp.float32) * SCALE
        kvb[0:TOK, pl.ds(narrow, HEAD)] = dk.astype(jnp.bfloat16)
        kvb[0:TOK, pl.ds(pl.multiple_of(KV + g * HEAD, HEAD), HEAD)] = dv.astype(jnp.bfloat16)
        return 0

    lax.fori_loop(0, GROUPS, group, 0)

    def kv_rows(kk, j):
        return pl.ds(kk * 256 + j * TOK, TOK)

    def kv_send(src, to, dst, n):
        return send(kvb.at[kv_rows(src, 0)], kvb.at[kv_rows(dst, 0)], kz_s.at[n], kz_r.at[dst], zdev[to])

    kz = {1: kv_send(0, 1, 1, 0), 3: kv_send(0, 3, 3, 1), 2: kv_send(3, 1, 2, 2)}
    kp = {1: kv_send(1, 3, 2, 3), 3: kz[2], 2: kv_send(2, 1, 3, 4)}
    kf = {kk: send(kvb.at[kv_rows(kk, 0)], kvb.at[kv_rows(kk, 1)], kf_s.at[kk], kf_r.at[kk], sib)
          for kk in range(4)}
    kz[1].start()

    @pl.when(middle)
    def _():
        kz[3].start()

    kf[0].start()
    for key in ((1, 1), (3, 0)):
        wc[key].start()

    for cp in hz:
        cp.wait_recv()
    hx = {(qq, n): send(hid.at[x, PART[n]], hid.at[x, PART[n]], hx_s.at[qq - 1, n], hx_r.at[qq - 1, n], xdev[qq])
          for qq, n in ((1, 0), (3, 1), (1, 1), (3, 0))}
    hx[2, 0] = send(hid.at[xor(x, 1), PART[0]], hid.at[xor(x, 1), PART[0]], hx_s.at[1, 0], hx_r.at[1, 0], xdev[3])
    hx[2, 1] = send(hid.at[xor(x, 3), PART[1]], hid.at[xor(x, 3), PART[1]], hx_s.at[1, 1], hx_r.at[1, 1], xdev[1])
    for key in ((1, 0), (3, 1)):
        hx[key].start()

    def tile(kk, r):
        t = lax.dot_general(kvb[kk * 256:(kk + 1) * 256], wb[r], NT, preferred_element_type=jnp.float32)
        st[kk, r] = t.astype(jnp.bfloat16)
        b, i, a, i2 = kk // 2, kk % 2, r % 2, r // 2
        qq = 2 * xor(ta, a) + xor(tb, b)

        @pl.when(qq != 0)
        def _():
            send(st.at[kk, r], rs.at[qq - 1, i, i2], x_s.at[qq - 1, i, i2], x_r.at[qq - 1, i, i2],
                 dev(y, z, c, h, xor(x, qq))).start()

    def finish(b, i):
        @pl.when(tb == b)
        def _():
            for i2 in range(2):
                finish_tile(i, i2)

    def finish_tile(i, i2):
        for n in range(3):
            send(rs.at[n, i, i2], rs.at[n, i, i2], x_s.at[n, i, i2], x_r.at[n, i, i2], sib).wait_recv()
        t = st[2 * tb + i, ta + 2 * i2].astype(jnp.float32)
        for n in range(3):
            t = t + rs[n, i, i2].astype(jnp.float32)
        fs[i, i2] = t.astype(jnp.bfloat16)
        g = xor(xor(y1, i2), h)
        for j in range(2):
            src = fs.at[i, i2, pl.ds(j * TOK, TOK)]
            to = last(i, i2, j)
            if i == 0 and j == 0:
                me = jnp.logical_and(aligned, g == 0)

                @pl.when(me)
                def _():
                    pltpu.make_async_copy(src, fin.at[g, i, j], f_r.at[g, i, j]).start()

                @pl.when(jnp.logical_not(me))
                def _():
                    send(src, fin.at[g, i, j], f_s.at[i, i2, j], f_r.at[g, i, j], to).start()
            else:
                send(src, fin.at[g, i, j], f_s.at[i, i2, j], f_r.at[g, i, j], to).start()

    wc[1, 0].wait_recv()
    wc[2, 0].start()
    wc[3, 1].wait_recv()
    wc[2, 1].start()
    for key in ((1, 1), (3, 0)):
        hx[key].start()
    kf[0].wait_recv()
    tile(0, 0)
    kz[1].wait_recv()

    @pl.when(middle)
    def _():
        kp[1].start()
        kz[3].wait_recv()
        kp[3].start()
        kf[3].start()

    kf[1].start()
    for key, nxt in (((1, 0), (2, 0)), ((3, 1), (2, 1))):
        hx[key].wait_recv()
        hx[nxt].start()
    for r, n in ((1, 1), (3, 0)):
        wc[r, n].wait_recv()
        tile(0, r)
    kf[1].wait_recv()
    for r in (0, 1, 3):
        tile(1, r)
    kz[2].wait_recv()

    @pl.when(middle)
    def _():
        kp[2].start()

    kf[2].start()
    for n in range(2):
        wc[2, n].wait_recv()
    tile(0, 2)
    tile(1, 2)
    kf[2].wait_recv()
    for r in (2, 1, 3, 0):
        tile(2, r)

    @pl.when(jnp.logical_not(middle))
    def _():
        kz[3].wait_recv()
        kf[3].start()

    kf[3].wait_recv()
    for r in (2, 1, 3, 0):
        tile(3, r)
    for key in ((1, 1), (3, 0), (2, 0), (2, 1)):
        hx[key].wait_recv()
    for cp in hc:
        cp.wait_recv()
    for cp in loads[5:9]:
        cp.wait()
    for r in range(4):
        hid_t[r] = hid[r].T

    def weight(r):
        return jnp.dot(hid_t[r], kvb[...], preferred_element_type=jnp.float32)

    g2 = [send(gs2.at[HALF[n]], gr2.at[n], g2_s.at[n], g2_r.at[n], ydev[3 if n else 1]) for n in range(2)]
    gc = {(r, n): send(gsend.at[r // 2, HALF[n]], grecv.at[r // 2, HALF[n]], g_s.at[r // 2, n], g_r.at[r // 2, n],
                       ydev[r]) for r in (1, 3) for n in range(2)}
    gs2[...] = weight(2).astype(jnp.bfloat16)
    for cp in g2:
        cp.start()
    t = weight(1)
    gsend[0, 0:128] = t[0:128].astype(jnp.bfloat16)
    keep[0] = t[128:256]
    gc[1, 0].start()
    t = weight(3)
    gsend[1, 128:256] = t[128:256].astype(jnp.bfloat16)
    keep[1] = t[0:128]
    gc[3, 1].start()
    finish(0, 0)
    finish(0, 1)
    finish(1, 0)
    own[...] = weight(0)
    g2[0].wait_recv()
    gsend[1, 0:128] = (keep[1] + gr2[0].astype(jnp.float32)).astype(jnp.bfloat16)
    gc[3, 0].start()
    g2[1].wait_recv()
    gsend[0, 128:256] = (keep[0] + gr2[1].astype(jnp.float32)).astype(jnp.bfloat16)
    gc[1, 1].start()

    finish(1, 1)
    for i in range(2):
        for j in range(2):
            for g in range(2):
                send(fin.at[g, i, j], fin.at[g, i, j], f_s.at[0, 0, 0], f_r.at[g, i, j], sib).wait_recv()
            t = fin[0, i, j].astype(jnp.float32) + fin[1, i, j].astype(jnp.float32)
            gh[:, pl.ds(pl.multiple_of(xor(z0, i) * 512 + xor(c, j) * 256, 256), 256)] = t.astype(jnp.bfloat16)

    for cp in gc.values():
        cp.wait_recv()
    gw[0] = (own[...] + grecv[0].astype(jnp.float32) + grecv[1].astype(jnp.float32)).astype(jnp.bfloat16)

    for cp in hz + hc + g2 + list(wc.values()) + list(hx.values()) + list(gc.values()):
        cp.wait_send()
    kz[1].wait_send()

    @pl.when(middle)
    def _():
        kz[3].wait_send()
        for kk in (1, 2, 3):
            kp[kk].wait_send()

    for kk in range(4):
        kf[kk].wait_send()
    for i in range(2):
        for i2 in range(2):
            for n in range(3):
                send(rs.at[n, i, i2], rs.at[n, i, i2], x_s.at[n, i, i2], x_r.at[n, i, i2], sib).wait_send()
            for j in range(2):
                cp = send(fs.at[i, i2, pl.ds(j * TOK, TOK)], fin.at[0, 0, 0], f_s.at[i, i2, j], f_r.at[0, 0, 0], sib)
                if i == 0 and j == 0:
                    @pl.when(jnp.logical_not(jnp.logical_and(aligned, xor(y1, i2) == h)))
                    def _():
                        cp.wait_send()
                else:
                    cp.wait_send()


def local(hidden, w_kv, queries, keys, values, out_grad, doc_lengths):
    bf, f32, dma = jnp.bfloat16, jnp.float32, pltpu.SemaphoreType.DMA
    vm, hbm = pl.BlockSpec(memory_space=pltpu.VMEM), pl.BlockSpec(memory_space=pltpu.HBM)
    return pl.pallas_call(
        body,
        out_shape=(jax.ShapeDtypeStruct((TOK, 1024), bf), jax.ShapeDtypeStruct((1, 256, KV2), bf)),
        in_specs=[hbm] * 7,
        out_specs=(vm, vm),
        scratch_shapes=[
            pltpu.SMEM((1, DOCS), jnp.int32),
            pltpu.VMEM((TOK, 4096), bf),
            pltpu.VMEM((TOK, KV), bf),
            pltpu.VMEM((TOK, KV), bf),
            pltpu.VMEM((TOK, 4096), bf),
            pltpu.VMEM((3, 2, TOK, 256), bf),
            pltpu.VMEM((4, 1024, 256), bf),
            pltpu.VMEM((4, 256, 1024), bf),
            pltpu.VMEM((4, 256, KV2), bf),
            pltpu.VMEM((1024, KV2), bf),
            pltpu.VMEM((4, 4, 256, 256), bf),
            pltpu.VMEM((3, 2, 2, 256, 256), bf),
            pltpu.VMEM((256, KV2), f32),
            pltpu.VMEM((2, 128, KV2), f32),
            pltpu.VMEM((256, KV2), bf),
            pltpu.VMEM((2, 128, KV2), bf),
            pltpu.VMEM((2, 256, KV2), bf),
            pltpu.VMEM((2, 256, KV2), bf),
            pltpu.VMEM((2, 2, 256, 256), bf),
            pltpu.VMEM((2, 2, 2, TOK, 256), bf),
            dma((3, 2)), dma((3, 2)), dma((4,)), dma((4,)), dma((3, 2)), dma((3, 2)), dma((3, 2)), dma((3, 2)),
            dma((5,)), dma((4,)), dma((4,)), dma((4,)),
            dma((3, 2, 2)), dma((3, 2, 2)),
            dma((2, 2)), dma((2, 2)), dma((2,)), dma((2,)), dma((2, 2, 2)), dma((2, 2, 2)), dma((16,)),
        ],
        compiler_params=pltpu.CompilerParams(
            collective_id=0, has_side_effects=True, vmem_limit_bytes=60 * 2**20),
        cost_estimate=pl.CostEstimate(flops=5 * 10**9, bytes_accessed=8 * 2**20, transcendentals=2**19),
    )(doc_lengths, hidden, w_kv, queries, keys, values, out_grad)


def solution(mesh):
    return jax.shard_map(
        local,
        mesh=mesh,
        in_specs=(
            P("dp", None),
            P("layer", "dp", None),
            P("layer", "dp", None),
            P("layer", "dp", None),
            P("layer", "dp", None),
            P("layer", "dp", None),
            P("dp", None),
        ),
        out_specs=(P("dp", "layer"), P("layer", "dp", None)),
        check_vma=False,
    )
```

time: 88.5 us -> 75.2 us (0.85)
  Pallas kernels: 78.5 us -> 70.9 us
  local copies, waits for them, and re-layouts: 9.03 us -> 3.54 us
    pallas_call x1, Pallas kernels: 78.5 us -> 70.9 us  [local(): pl.pallas_call(body, out_shape=(jax.ShapeDtypeStruct((TOK, 1024), bf), ja...]
    unnamed x16 -> x2, local copies, waits for them, and re-layouts: 9.03 us -> 3.54 us
where the time goes in v2:
time: 75.2 us; the launch traced here: 75.1 us
  Pallas kernels  70.9 us (94%)
  local copies, waits for them, and re-layouts  3.54 us (5%)
    pallas_call x1, Pallas kernels, local(): pl.pallas_call(body, out_shape=(jax.ShapeDtypeStruct((TOK, 1024), bf), ja...  70.9 us
    unnamed x2, local copies, waits for them, and re-layouts  3.54 us

profile of v2, /device:TPU:19, one launch (start us, length us, event | category | flops | bytes accessed | tf_op | source)
XLA Modules:
  0.0 75.1 jit_solution(5563504196879227460)
XLA Ops:
  0.6 70.9 %shard_map.86 = (bf16[128,1024]{1,0:T(8,128)(2,1)}, bf16[1,256,1024]{2,1,0:T(8,128)(2,1)}) custom-call(s32[1,8]{1,0:T(1,128)} %lens_in.1, bf16[128,8192]{1,0:T(8,128)(2,1)} %hidden.1, bf16[1,256,1024]{2,1,0:T(8,128)(2,1)} %w.1, bf16[1,128,4096]{2,1,0:T(8,128)(2,1)} %q_in.1, bf16[1,128,512]{2,1,0:T(8,128)(2,1)} %k_in.1, bf16[1,128,512]{2,1,0:T(8,128)(2,1)} %v_in.1, ...), custom_call_target="tpu_custom_call" | custom-call | flops 5000000000 | bytes 8388608 | tf_op jit(solution)/shard_map/pallas_call | solution.py:359
  71.5 1.7 %copy.11 = bf16[128,1024]{1,0:T(8,128)(2,1)} copy(bf16[128,1024]{1,0:T(8,128)(2,1)} %get-tuple-element.4) | data formatting | bytes 524288
  73.2 1.9 %copy.12 = bf16[1,256,1024]{2,1,0:T(8,128)(2,1)} copy(bf16[1,256,1024]{2,1,0:T(8,128)(2,1)} %get-tuple-element.5) | data formatting | bytes 1048576

commit v3 on v2

--- a/solution.py
+++ b/solution.py
@@ -162,30 +162,27 @@
         return pl.ds(kk * 256 + j * TOK, TOK)
 
     def kv_send(src, to, dst, n):
-        return send(kvb.at[kv_rows(src, 0)], kvb.at[kv_rows(dst, 0)], kz_s.at[n], kz_r.at[dst], zdev[to])
+        return [send(kvb.at[pl.ds(src * 256 + m * 64, 64)], kvb.at[pl.ds(dst * 256 + m * 64, 64)],
+                     kz_s.at[n, m], kz_r.at[dst, m], zdev[to]) for m in range(2)]
 
     kz = {1: kv_send(0, 1, 1, 0), 3: kv_send(0, 3, 3, 1), 2: kv_send(3, 1, 2, 2)}
     kp = {1: kv_send(1, 3, 2, 3), 3: kz[2], 2: kv_send(2, 1, 3, 4)}
     kf = {kk: send(kvb.at[kv_rows(kk, 0)], kvb.at[kv_rows(kk, 1)], kf_s.at[kk], kf_r.at[kk], sib)
           for kk in range(4)}
-    kz[1].start()
-
-    @pl.when(middle)
-    def _():
-        kz[3].start()
+    for m in range(2):
+        kz[1][m].start()
+
+        @pl.when(middle)
+        def _():
+            kz[3][m].start()
 
     kf[0].start()
     for key in ((1, 1), (3, 0)):
         wc[key].start()
-
-    for cp in hz:
-        cp.wait_recv()
     hx = {(qq, n): send(hid.at[x, PART[n]], hid.at[x, PART[n]], hx_s.at[qq - 1, n], hx_r.at[qq - 1, n], xdev[qq])
           for qq, n in ((1, 0), (3, 1), (1, 1), (3, 0))}
     hx[2, 0] = send(hid.at[xor(x, 1), PART[0]], hid.at[xor(x, 1), PART[0]], hx_s.at[1, 0], hx_r.at[1, 0], xdev[3])
     hx[2, 1] = send(hid.at[xor(x, 3), PART[1]], hid.at[xor(x, 3), PART[1]], hx_s.at[1, 1], hx_r.at[1, 1], xdev[1])
-    for key in ((1, 0), (3, 1)):
-        hx[key].start()
 
     def tile(kk, r):
         t = lax.dot_general(kvb[kk * 256:(kk + 1) * 256], wb[r], NT, preferred_element_type=jnp.float32)
@@ -201,8 +198,8 @@
     def finish(b, i):
         @pl.when(tb == b)
         def _():
-            for i2 in range(2):
-                finish_tile(i, i2)
+            for far in (1, 0):
+                finish_tile(i, xor(xor(y1, h), far))
 
     def finish_tile(i, i2):
         for n in range(3):
@@ -228,38 +225,61 @@
             else:
                 send(src, fin.at[g, i, j], f_s.at[i, i2, j], f_r.at[g, i, j], to).start()
 
+    def hidden_on(keys):
+        for key in keys:
+            hx[key].start()
+
+    def hidden_in():
+        for cp in hz:
+            cp.wait_recv()
+        hidden_on(((1, 0), (3, 1)))
+
+    def hidden_pass():
+        for key, nxt in (((1, 0), (2, 0)), ((3, 1), (2, 1))):
+            hx[key].wait_recv()
+            hx[nxt].start()
+
+    def kv_pass(m):
+        @pl.when(middle)
+        def _():
+            for kk in (1, 3):
+                kz[kk][m].wait_recv()
+                kp[kk][m].start()
+
+    hidden_in()
+    hidden_on(((1, 1), (3, 0)))
+    hidden_pass()
     wc[1, 0].wait_recv()
     wc[2, 0].start()
     wc[3, 1].wait_recv()
     wc[2, 1].start()
-    for key in ((1, 1), (3, 0)):
-        hx[key].start()
     kf[0].wait_recv()
     tile(0, 0)
-    kz[1].wait_recv()
+    kv_pass(0)
+    kv_pass(1)
 
     @pl.when(middle)
     def _():
-        kp[1].start()
-        kz[3].wait_recv()
-        kp[3].start()
         kf[3].start()
 
+    @pl.when(jnp.logical_not(middle))
+    def _():
+        for m in range(2):
+            kz[1][m].wait_recv()
+
     kf[1].start()
-    for key, nxt in (((1, 0), (2, 0)), ((3, 1), (2, 1))):
-        hx[key].wait_recv()
-        hx[nxt].start()
     for r, n in ((1, 1), (3, 0)):
         wc[r, n].wait_recv()
         tile(0, r)
     kf[1].wait_recv()
     for r in (0, 1, 3):
         tile(1, r)
-    kz[2].wait_recv()
-
-    @pl.when(middle)
-    def _():
-        kp[2].start()
+    for m in range(2):
+        kz[2][m].wait_recv()
+
+        @pl.when(middle)
+        def _():
+            kp[2][m].start()
 
     kf[2].start()
     for n in range(2):
@@ -272,7 +292,8 @@
 
     @pl.when(jnp.logical_not(middle))
     def _():
-        kz[3].wait_recv()
+        for m in range(2):
+            kz[3][m].wait_recv()
         kf[3].start()
 
     kf[3].wait_recv()
@@ -329,13 +350,14 @@
 
     for cp in hz + hc + g2 + list(wc.values()) + list(hx.values()) + list(gc.values()):
         cp.wait_send()
-    kz[1].wait_send()
-
-    @pl.when(middle)
-    def _():
-        kz[3].wait_send()
-        for kk in (1, 2, 3):
-            kp[kk].wait_send()
+    for m in range(2):
+        kz[1][m].wait_send()
+
+        @pl.when(middle)
+        def _():
+            kz[3][m].wait_send()
+            for kk in (1, 2, 3):
+                kp[kk][m].wait_send()
 
     for kk in range(4):
         kf[kk].wait_send()
@@ -383,7 +405,7 @@
             pltpu.VMEM((2, 2, 256, 256), bf),
             pltpu.VMEM((2, 2, 2, TOK, 256), bf),
             dma((3, 2)), dma((3, 2)), dma((4,)), dma((4,)), dma((3, 2)), dma((3, 2)), dma((3, 2)), dma((3, 2)),
-            dma((5,)), dma((4,)), dma((4,)), dma((4,)),
+            dma((5, 2)), dma((4, 2)), dma((4,)), dma((4,)),
             dma((3, 2, 2)), dma((3, 2, 2)),
             dma((2, 2)), dma((2, 2)), dma((2,)), dma((2,)), dma((2, 2, 2)), dma((2, 2, 2)), dma((16,)),
         ],

time: 75.2 us -> 75.4 us (level)
  no operation moved by 1% of the time
where the time goes in v3:
time: 75.4 us; the launch traced here: 75.1 us
  Pallas kernels  71 us (94%)
  local copies, waits for them, and re-layouts  3.54 us (5%)
    pallas_call x1, Pallas kernels, local(): pl.pallas_call(body, out_shape=(jax.ShapeDtypeStruct((TOK, 1024), bf), ja...  71 us
    unnamed x2, local copies, waits for them, and re-layouts  3.54 us

profile of v3, /device:TPU:19, one launch (start us, length us, event | category | flops | bytes accessed | tf_op | source)
XLA Modules:
  0.0 75.1 jit_solution(14087385903427688751)
XLA Ops:
  0.6 71.0 %shard_map.86 = (bf16[128,1024]{1,0:T(8,128)(2,1)}, bf16[1,256,1024]{2,1,0:T(8,128)(2,1)}) custom-call(s32[1,8]{1,0:T(1,128)} %lens_in.1, bf16[128,8192]{1,0:T(8,128)(2,1)} %hidden.1, bf16[1,256,1024]{2,1,0:T(8,128)(2,1)} %w.1, bf16[1,128,4096]{2,1,0:T(8,128)(2,1)} %q_in.1, bf16[1,128,512]{2,1,0:T(8,128)(2,1)} %k_in.1, bf16[1,128,512]{2,1,0:T(8,128)(2,1)} %v_in.1, ...), custom_call_target="tpu_custom_call" | custom-call | flops 5000000000 | bytes 8388608 | tf_op jit(solution)/shard_map/pallas_call | solution.py:381
  71.6 1.7 %copy.11 = bf16[128,1024]{1,0:T(8,128)(2,1)} copy(bf16[128,1024]{1,0:T(8,128)(2,1)} %get-tuple-element.4) | data formatting | bytes 524288
  73.3 1.9 %copy.12 = bf16[1,256,1024]{2,1,0:T(8,128)(2,1)} copy(bf16[1,256,1024]{2,1,0:T(8,128)(2,1)} %get-tuple-element.5) | data formatting | bytes 1048576
